TPU v7x, 256 devices: a whole 4x4x8 slice. The times are simulated.
256 devices in a mesh: span: 4 (over z_hi, core), head: 16 (over z_lo, x), rep: 4 (over y).
Axes of the slice: x: 4, y: 4, z: 8 (z_hi: 2, z_lo: 4; z = z_hi * 4 + z_lo), core: 2. Of those that a mesh axis runs over, the one named last changes fastest.
Arguments:
- queries: bfloat16 [16384, 6144], P(('rep', 'span', 'head')), parts along dimension 0, may hold values from -10 to 10
- key_value: bfloat16 [16384, 2, 1024], P(('rep', 'span', 'head')), parts along dimension 0, may hold values from -4 to 4
- w_out: bfloat16 [6144, 6144], P('head'), may hold values from -0.078125 to 0.078125
- gate_table: bfloat16 [64, 6144], replicated, may hold values from 0.25 to 2
- levels: int32 [16], P('rep'), parts along dimension 0, may hold values from 0 to 63
- span_mask: int32 [16, 4], P('rep'), parts along dimension 0, may hold values from 0 to 1, as said below
- counts: int32 [16], P('rep'), parts along dimension 0, may hold values from 512 to 1024, as said below
Outputs:
- output: bfloat16 [16384, 6144], P(('rep', 'span', 'head')), parts along dimension 0
There are 4 independent parts, one for each index of `rep`. A program takes and returns all parts, laid end to end along the dimension named above; an argument that names none is the same for every part. Nothing has to cross between parts.
Inputs may be any that keep to these rules, and one draw needn't show every extreme that they name: span_mask[i, i] = 1 and span_mask[i, i - 1] = 1; span_mask[i, j] = 0 for j > i; the entries for j < i - 1 are drawn. `counts`: in every video one span has exactly 1024 live tokens and another exactly 512.
All inputs are finite; a program needn't handle non-finite values.
Results may differ from a plain program's by a relative error of at most 0.024.
Values may be sent and summed in bfloat16 or wider, within the bound.
A program may use at most 64 MiB of HBM per device.

v0:
```python
import jax
import jax.numpy as jnp
from jax import lax
from jax.sharding import PartitionSpec as P

HEADS = 48
HD = 128
KV_GROUPS = 8


NEG_FILL = -1e30


def key_usable(key_span, key_pos, own_span, span_mask, counts):
    span_ids = jnp.arange(span_mask.shape[0], dtype=jnp.int32)
    own_row = jnp.sum(jnp.where((span_ids == own_span)[:, None], span_mask, 0), axis=0)
    span_hits = key_span[:, None] == span_ids[None, :]
    allowed = jnp.sum(jnp.where(span_hits, own_row[None, :], 0), axis=1)
    row_limit = jnp.sum(jnp.where(span_hits, counts[None, :], 0), axis=1)
    return (allowed > 0) & (key_pos < row_limit)


def attend(status, local_queries, key_block, usable):
    maxima, totals, weighted = status
    head_count = maxima.shape[0]
    head_width = local_queries.shape[1] // head_count
    score_scale = head_width ** (-0.5)
    key_rows = key_block[:, 0]
    value_rows = key_block[:, 1]

    def one_head(head_id, running):
        maxima, totals, weighted = running
        query = lax.dynamic_slice_in_dim(local_queries, head_id * head_width, head_width, 1)
        scores = (
            lax.dot_general(
                query, key_rows, (((1,), (1,)), ((), ())), preferred_element_type=jnp.float32
            )
            * score_scale
        )
        scores = jnp.where(usable[None, :], scores, NEG_FILL)
        earlier_max = lax.dynamic_index_in_dim(maxima, head_id, 0, keepdims=False)
        latest = jnp.maximum(earlier_max, jnp.max(scores, axis=1))
        weights = jnp.where(usable[None, :], jnp.exp(scores - latest[:, None]), 0.0)
        factor = jnp.exp(earlier_max - latest)
        earlier_total = lax.dynamic_index_in_dim(totals, head_id, 0, keepdims=False)
        new_total = earlier_total * factor + jnp.sum(weights, axis=1)
        partial_value = jnp.dot(
            weights.astype(jnp.bfloat16), value_rows, preferred_element_type=jnp.float32
        )
        previous = lax.dynamic_slice_in_dim(weighted, head_id * head_width, head_width, 1)
        weighted = lax.dynamic_update_slice_in_dim(
            weighted, previous * factor[:, None] + partial_value, head_id * head_width, 1
        )
        maxima = maxima.at[head_id].set(latest)
        totals = totals.at[head_id].set(new_total)
        return (maxima, totals, weighted)

    return lax.fori_loop(0, head_count, one_head, status)


def absorb(status, local_queries, key_block, usable):
    return attend(status, local_queries, key_block, usable)


def starting(local_queries):
    span_len = local_queries.shape[0]
    head_count = local_queries.shape[1] // HD
    return (
        jnp.full((head_count, span_len), NEG_FILL, jnp.float32),
        jnp.zeros((head_count, span_len), jnp.float32),
        jnp.zeros(local_queries.shape, jnp.float32),
    )


def local(queries, key_value, w_out, gate_table, levels, span_mask, counts):
    tok_rows = queries.shape[0]
    own_span = lax.axis_index("span")
    own_shard = lax.axis_index("head")
    shard_count = lax.axis_size("head")
    head_count = HEADS // shard_count
    share = HEADS // KV_GROUPS
    copies = max(1, share // head_count)
    query_rows = queries.reshape(tok_rows, 1, queries.shape[1])
    gathered = lax.all_gather(key_value, "span", axis=0, tiled=True)
    row_total = gathered.shape[0]
    split = gathered.reshape(row_total, 2, KV_GROUPS, 1, HD)
    spread = jnp.broadcast_to(split, (row_total, 2, KV_GROUPS, copies, HD))
    query_part = lax.all_to_all(query_rows, "head", split_axis=2, concat_axis=0, tiled=True)
    key_all = lax.all_to_all(
        spread.reshape(row_total, 2, KV_GROUPS * copies * HD),
        "head",
        split_axis=2,
        concat_axis=0,
        tiled=True,
    )
    local_queries = query_part[:, 0]
    span_count = lax.axis_size("span")
    group_width = key_all.shape[2]
    grouped = key_all.reshape(shard_count, span_count, tok_rows, 2, group_width)
    status = starting(local_queries)
    key_pos = jnp.arange(shard_count * tok_rows, dtype=jnp.int32)
    for source in range(span_count):
        key_block = grouped[:, source].reshape(shard_count * tok_rows, 2, group_width)
        key_span = jnp.full((shard_count * tok_rows,), source, jnp.int32)
        usable = key_usable(key_span, key_pos, own_span, span_mask, counts)
        status = absorb(status, local_queries, key_block, usable)
    maxima, totals, weighted = status
    span_len = local_queries.shape[0]
    divided = weighted.reshape(span_len, head_count, HD) / jnp.transpose(totals)[:, :, None]
    attended = divided.reshape(span_len, head_count * HD).astype(jnp.bfloat16)
    summed = lax.psum_scatter(
        jnp.dot(attended, w_out, preferred_element_type=jnp.float32).astype(jnp.bfloat16),
        "head",
        scatter_dimension=0,
        tiled=True,
    ).astype(jnp.float32)
    span_ids = jnp.arange(levels.shape[0], dtype=jnp.int32)
    noise_level = jnp.sum(jnp.where(span_ids == own_span, levels, 0))
    own_count = jnp.sum(jnp.where(span_ids == own_span, counts, 0))
    selector = (jnp.arange(gate_table.shape[0], dtype=jnp.int32) == noise_level).astype(
        jnp.bfloat16
    )
    gate_row = jnp.dot(selector[None, :], gate_table, preferred_element_type=jnp.float32)
    positions = own_shard * tok_rows + jnp.arange(tok_rows, dtype=jnp.int32)
    return jnp.where((positions < own_count)[:, None], summed * gate_row, 0.0).astype(jnp.bfloat16)


def solution(mesh):
    in_specs = (
        P(("rep", "span", "head"), None),
        P(("rep", "span", "head"), None, None),
        P("head", None),
        P(),
        P("rep"),
        P("rep", None),
        P("rep"),
    )
    out_specs = P(("rep", "span", "head"), None)
    return jax.shard_map(local, mesh=mesh, in_specs=in_specs, out_specs=out_specs, check_vma=False)
```

profile of v0, /device:TPU:1, one launch (start us, length us, event | category | flops | bytes accessed | tf_op | source)
XLA Modules:
  0.0 389.7 jit_solution(7248465946643193718)
XLA Ops:
  7.3 7.3 %copy.51 = bf16[64,1,6144]{0,1,2:T(2,128)(2,1)} copy(bf16[64,1,6144]{2,0,1:T(8,128)(2,1)} %bitcast.148) | data formatting | bytes 1572864 | tf_op jit(solution)/shard_map/reshape | solution.py:83
  15.0 34.3 %reduce.60 = bf16[6144,64]{1,0:T(8,128)(2,1)S(1)} reduce(bf16[6144,1,64]{2,1,0:T(2,128)(2,1)} %bitcast.123, bf16[]{:T(256)} %broadcast.287), dimensions={1}, to_apply=%bitcast.61.reduce_sub_computation | reduce | bytes 1572866
  49.4 1.9 reshape.509
  51.3 9.0 %all-to-all-start = ((bf16[16,2,12288]{2,1,0:T(2,128)(2,1)}), bf16[16,2,12288]{2,1,0:T(2,128)(2,1)S(1)}, u32[]{:S(2)}, u32[]{:S(2)}) async-start(bf16[16,2,12288]{2,1,0:T(2,128)(2,1)} %reshape.509), calls=%async_computation | async-start | bytes 1572864 | tf_op jit(solution)/shard_map/all_to_all | solution.py:88
  60.3 4.4 %copy.62 = bf16[256,2,1024]{0,1,2:T(2,128)(2,1)S(1)} copy(bf16[256,2,1024]{2,1,0:T(2,128)(2,1)} %all-gather.2.cloned.1.call-done) | data formatting | bytes 2097152 | tf_op jit(solution)/shard_map/broadcast_in_dim | solution.py:87
  64.7 13.7 %all-to-all-done = bf16[16,2,12288]{2,1,0:T(2,128)(2,1)S(1)} async-done(((bf16[16,2,12288]{2,1,0:T(2,128)(2,1)}), bf16[16,2,12288]{2,1,0:T(2,128)(2,1)S(1)}, u32[]{:S(2)}, u32[]{:S(2)}) %all-to-all-start) | async-done | bytes 786464 | tf_op jit(solution)/shard_map/all_to_all | solution.py:88
  78.4 3.0 broadcast_in_dim.306
  81.4 6.2 %all-to-all-start.1 = ((bf16[256,2,2048]{0,1,2:T(2,128)(2,1)}), bf16[256,2,2048]{0,1,2:T(2,128)(2,1)}, u32[]{:S(2)}, u32[]{:S(2)}) async-start(bf16[256,2,2048]{0,1,2:T(2,128)(2,1)} %bitcast.125), calls=%async_computation.1 | async-start | bytes 4194304 | tf_op jit(solution)/shard_map/all_to_all | solution.py:89
  88.1 4.0 %reshape.510 = bf16[6144,1,64]{2,1,0:T(2,128)(2,1)} reshape(bf16[16,2,12288]{2,1,0:T(2,128)(2,1)S(1)} %all-to-all-done) | data formatting | bytes 1572864
  92.1 6.0 %copy.52 = bf16[64,1,6144]{2,0,1:T(8,128)(2,1)S(1)} copy(bf16[64,1,6144]{0,1,2:T(2,128)(2,1)} %bitcast.124) | data formatting | bytes 1572864 | tf_op jit(solution)/shard_map/all_to_all | solution.py:88
  98.5 30.6 %all-to-all-done.1 = bf16[256,2,2048]{0,1,2:T(2,128)(2,1)} async-done(((bf16[256,2,2048]{0,1,2:T(2,128)(2,1)}), bf16[256,2,2048]{0,1,2:T(2,128)(2,1)}, u32[]{:S(2)}, u32[]{:S(2)}) %all-to-all-start.1) | async-done | bytes 2097184 | tf_op jit(solution)/shard_map/all_to_all | solution.py:89
  129.1 3.2 copy.55
  132.3 4.0 %copy.56 = bf16[16,256,2,128]{3,1,2,0:T(8,128)(2,1)} copy(bf16[16,256,2,128]{1,3,0,2:T(8,128)(2,1)} %bitcast.127) | data formatting | bytes 4194304 | tf_op jit(solution)/shard_map/all_to_all | solution.py:89
  136.3 2.8 fusion.90
  139.9 16.9 %while.76 = (s32[]{:T(128)}, f32[3,1024]{1,0:T(4,128)S(1)}, f32[3,1024]{1,0:T(4,128)S(1)}, f32[1024,384]{1,0:T(8,128)S(1)}, pred[1024]{0:T(1024)(128)(4,1)S(1)},...) while((s32[]{:T(128)}, f32[3,1024]{1,0:T(4,128)S(1)}, ...), condition=%wide.region_8.9_spmd, body=%wide.region_4.0_spmd.sunk | while | flops 550771712 | bytes 15559930 | solution.py:58
  142.1 1.5 fusion.131
  147.8 1.5 fusion.131
  153.4 1.5 fusion.131
  158.7 16.9 %while.77 = (s32[]{:T(128)}, f32[3,1024]{1,0:T(4,128)S(1)}, f32[3,1024]{1,0:T(4,128)S(1)}, f32[1024,384]{1,0:T(8,128)S(1)}, pred[1024]{0:T(1024)(128)(4,1)S(1)},...) while((s32[]{:T(128)}, f32[3,1024]{1,0:T(4,128)S(1)}, ...), condition=%wide.region_15.16_spmd, body=%wide.region_11.15_spmd.sunk | while | flops 550771712 | bytes 15559930 | solution.py:58
  166.5 1.5 fusion.137
  172.1 1.5 fusion.137
  177.3 16.9 %while.78 = (s32[]{:T(128)}, f32[3,1024]{1,0:T(4,128)S(1)}, f32[3,1024]{1,0:T(4,128)S(1)}, f32[1024,384]{1,0:T(8,128)S(1)}, pred[1024]{0:T(1024)(128)(4,1)S(1)},...) while((s32[]{:T(128)}, f32[3,1024]{1,0:T(4,128)S(1)}, ...), condition=%wide.region_22.23_spmd, body=%wide.region_18.22_spmd.sunk | while | flops 550771712 | bytes 15559930 | solution.py:58
  185.2 1.5 fusion.143
  190.8 1.5 fusion.143
  196.0 17.4 %while.79 = (s32[]{:T(128)}, f32[3,1024]{1,0:T(4,128)S(1)}, f32[3,1024]{1,0:T(4,128)S(1)}, f32[1024,384]{1,0:T(8,128)S(1)}, pred[1024]{0:T(1024)(128)(4,1)S(1)},...) while((s32[]{:T(128)}, f32[3,1024]{1,0:T(4,128)S(1)}, ...), condition=%wide.region_29.30_spmd, body=%wide.region_25.0_spmd.sunk | while | flops 550771712 | bytes 15559930 | solution.py:58
  204.1 1.5 fusion.149
  209.9 1.5 fusion.149
  213.4 1.6 copy.61
  215.0 1.6 fusion.80
  216.6 12.0 %convolution_convert_fusion = bf16[1024,6144]{1,0:T(8,128)(2,1)} fusion(bf16[1024,384]{0,1:T(8,128)(2,1)S(1)} %fusion.80, bf16[384,6144]{1,0:T(8,128)(2,1)} %param.33), kind=kOutput, calls=%fused_computation.92 | convolution fusion | flops 4838129664 | bytes 18087936 | tf_op jit(solution)/shard_map/dot_general | solution.py:112
  231.4 149.3 %reduce-scatter.2.cloned.1.call-done = bf16[64,6144]{1,0:T(8,128)(2,1)} async-done(((bf16[1024,6144]{1,0:T(8,128)(2,1)}), bf16[64,6144]{1,0:T(8,128)(2,1)}) %reduce-scatter.2.cloned.1.call-update) | async-done | bytes 786448 | tf_op jit(solution)/shard_map/reduce_scatter | solution.py:111
  380.7 2.2 select_convert_fusion
  (165 shorter events, 64.2 us)
Async XLA Ops:
  6.5 224.0 %copy-start = (bf16[64,6144]{1,0:T(8,128)(2,1)S(1)}, bf16[64,6144]{1,0:T(8,128)(2,1)}, u32[]{:S(2)}) copy-start(bf16[64,6144]{1,0:T(8,128)(2,1)} %param.34) | copy-start | bytes 2359300
  6.5 53.8 %all-gather.2.cloned.1.call-start = ((), (), s32[]{:S(2)}) async-start(), calls=%async_computation.3 | async-start | bytes 1310720 | tf_op jit(solution)/shard_map/all_gather | solution.py:84
  51.3 27.1 %all-to-all-start = ((bf16[16,2,12288]{2,1,0:T(2,128)(2,1)}), bf16[16,2,12288]{2,1,0:T(2,128)(2,1)S(1)}, u32[]{:S(2)}, u32[]{:S(2)}) async-start(bf16[16,2,12288]{2,1,0:T(2,128)(2,1)} %reshape.509), calls=%async_computation | async-start | bytes 1572864 | tf_op jit(solution)/shard_map/all_to_all | solution.py:88
  64.7 23.2 %copy-start.6 = (s32[4,4]{1,0:T(4,128)S(1)}, s32[4,4]{1,0:T(4,128)}, u32[]{:S(2)}) copy-start(s32[4,4]{1,0:T(4,128)} %param.36) | copy-start | bytes 196
  64.7 23.3 %copy-start.7 = (s32[4]{0:T(128)S(1)}, s32[4]{0:T(128)}, u32[]{:S(2)}) copy-start(s32[4]{0:T(128)} %param.37) | copy-start | bytes 52
  81.4 47.7 %all-to-all-start.1 = ((bf16[256,2,2048]{0,1,2:T(2,128)(2,1)}), bf16[256,2,2048]{0,1,2:T(2,128)(2,1)}, u32[]{:S(2)}, u32[]{:S(2)}) async-start(bf16[256,2,2048]{0,1,2:T(2,128)(2,1)} %bitcast.125), calls=%async_computation.1 | async-start | bytes 4194304 | tf_op jit(solution)/shard_map/all_to_all | solution.py:89
  87.6 293.1 %reduce-scatter.2.cloned.1.call-start = ((), (), s32[]{:S(2)}) async-start(), calls=%async_computation.4 | async-start | bytes 13369344 | tf_op jit(solution)/shard_map/reduce_scatter | solution.py:111
  136.3 3.7 copy-start.5
  139.9 2.2 copy-start.2
  145.6 2.2 copy-start.2
  151.2 2.2 copy-start.2
  158.7 2.2 copy-start.3
  164.3 2.2 copy-start.3
  169.9 2.2 copy-start.3
  177.3 2.2 copy-start.4
  183.0 2.2 copy-start.4
  188.6 2.2 copy-start.4
  196.0 2.3 copy-start.1
  201.8 2.3 copy-start.1
  207.6 2.3 copy-start.1
  228.6 1.3 copy-start.8
Sparse Core Ops, SparseCore 0:
  9.2 35.9 all-gather.1
  228.7 151.8 reduce-scatter.1
where the time goes:
time: 391 us; the launch traced here: 390 us
  waiting for transfers between devices  194 us (50%)
  other arithmetic  78.1 us (20%)
  local copies, waits for them, and re-layouts  47.1 us (12%)
  matrix products  40.2 us (10%)
  starting transfers between devices  15.4 us (4%)
  between operations  13.7 us (4%)
    reduce_scatter x1, waiting for transfers between devices, local(): lax.psum_scatter(jnp.dot(attended, w_out, preferred_element_type=jnp.floa...  149 us
    unnamed x1, other arithmetic  34.3 us
    all_to_all x1, waiting for transfers between devices, local(): lax.all_to_all(spread.reshape(row_total, 2, KV_GROUPS * copies * HD), 'he...  30.6 us
    another operation x36, other arithmetic  24.9 us
    dot_general x12, matrix products, one_head(): jnp.dot(weights.astype(jnp.bfloat16), value_rows, preferred_element_type=...  18.4 us
    all_to_all x1, waiting for transfers between devices, local(): lax.all_to_all(query_rows, 'head', split_axis=2, concat_axis=0, tiled=True)  13.7 us
    reduce_sum x12, other arithmetic, one_head(): new_total = earlier_total * factor + jnp.sum(weights, axis=1)  12.7 us
    dot_general x1, matrix products, local(): jnp.dot(attended, w_out, preferred_element_type=jnp.float32)  12 us
  transfers between devices with their start and end apart: 4, of which 3 were waited for; matrix products, arithmetic and copies ran while one was open for 16% of the time, Pallas kernels for 0%

commit v1 on v0

v1 whole, which is shorter than its diff:
```python
import jax
import jax.numpy as jnp
from jax import lax
from jax.experimental import pallas as pl
from jax.experimental.pallas import tpu as pltpu
from jax.sharding import PartitionSpec as P

MESH = pl.DeviceIdType.MESH
HD = 128
SPAN = 1024
D = 6144
ROWS = 64
QT = 256
SHARD = 384
ZC = 1024
QC = 1280
EXP_SCALE = HD**-0.5 * 1.4426950408889634
F32 = jnp.float32
BF16 = jnp.bfloat16


class Names:
    def __init__(self):
        self.ids = {}

    def __call__(self, name):
        return self.ids.setdefault(name, len(self.ids))


N_MESSAGES = 100
N_LOCAL = 8


def kernel(
    q_hbm, kv_hbm, w_hbm, gate_ref, levels_ref, mask_ref, counts_ref, out_ref,
    q_buf, kv_buf, kp, ve, m_ref, acc, a_st, a_buf, w_buf, o_st, ra_l, ra_r, rb_l, rb_r,
    gate_row, send_sem, recv_sem, local_sem,
):
    span = lax.axis_index("span")
    head = lax.axis_index("head")
    y = lax.axis_index("rep")
    core = lax.rem(span, 2)
    zl = head // 4
    x = lax.rem(head, 4)
    z = (span // 2) * 4 + zl
    a = x // 2
    b = lax.rem(x, 2)

    def at_x(xx):
        return {"head": zl * 4 + xx}

    def at_z(zz):
        return {"span": (zz // 4) * 2 + core, "head": lax.rem(zz, 4) * 4 + x}

    def at_y(yy):
        return {"rep": yy}

    sibling = {"span": (span // 2) * 2 + 1 - core}
    x_peers = [lax.rem(x + d, 4) for d in range(4)]
    z_right, z_left = lax.rem(z + 1, 8), lax.rem(z + 7, 8)
    y_right, y_left = lax.rem(y + 1, 4), lax.rem(y + 3, 4)
    y_far = lax.rem(y + 2, 4)

    names = Names()
    sent = []

    def message(name, src, dst, where):
        number = names(name)
        return pltpu.make_async_remote_copy(
            src_ref=src, dst_ref=dst, send_sem=send_sem.at[number], recv_sem=recv_sem.at[number],
            device_id=where, device_id_type=MESH,
        )

    def send(name, src, dst, where):
        message(name, src(), dst(), where()).start()
        sent.append((name, src, dst, where))

    def arrived(name, dst):
        message(name, dst, dst, sibling).wait_recv()

    barrier = pltpu.get_barrier_semaphore()
    peers = [at_x(x_peers[d]) for d in (1, 2, 3)]
    peers += [at_z(z_right), at_z(z_left), at_y(y_right), at_y(y_left), sibling]
    for peer in peers:
        pl.semaphore_signal(barrier, inc=1, device_id=peer, device_id_type=MESH)
    pl.semaphore_wait(barrier, len(peers))

    def group_of(xx, g):
        return 4 * lax.rem(xx, 2) + 2 * g + xx // 2

    def cols(start, width):
        return pl.ds(pl.multiple_of(start, 128), width)

    def rows(start, width):
        return pl.ds(pl.multiple_of(start, 64), width)

    def z_cols():
        return cols(core * (ZC // 2), ZC // 2)

    def q_cols(n):
        return cols(ZC + n * QC + core * (QC // 2), QC // 2)

    def z_cols_sib():
        return cols((1 - core) * (ZC // 2), ZC // 2)

    def q_cols_sib(n):
        return cols(ZC + n * QC + (1 - core) * (QC // 2), QC // 2)

    GROUPS = {"G1": (SHARD, 2 * SHARD), "G2": (3 * SHARD, SHARD)}

    def w_at(start, size, where):
        return w_buf.at[pl.ds(start, size), where()]

    def w_first(kind, where):
        send(kind + "R1", lambda: w_hbm.at[:, where()], lambda: w_at(SHARD, SHARD, where), lambda: at_z(z_right))
        send(kind + "L1", lambda: w_hbm.at[:, where()], lambda: w_at(2 * SHARD, SHARD, where), lambda: at_z(z_left))

    half = SHARD // 2

    def w_second(kind, where):
        arrived(kind + "R1", w_at(SHARD, SHARD, where))
        send(kind + "R2", lambda: w_at(SHARD, half, where), lambda: w_at(3 * SHARD, half, where), lambda: at_z(z_right))
        arrived(kind + "L1", w_at(2 * SHARD, SHARD, where))
        send(kind + "L2", lambda: w_at(2 * SHARD + half, half, where), lambda: w_at(3 * SHARD + half, half, where), lambda: at_z(z_left))

    def w_third(kind, where):
        arrived(kind + "R2", w_at(3 * SHARD, half, where))
        arrived(kind + "L2", w_at(3 * SHARD + half, half, where))

    def w_sibling(name, group, where):
        start, size = GROUPS[group]
        send("S" + name + group, lambda: w_at(start, size, where), lambda: w_at(start, size, where), lambda: sibling)

    def w_from_sibling(name, group, where):
        start, size = GROUPS[group]
        arrived("S" + name + group, w_at(start, size, where))

    def y_first(group):
        start, size = GROUPS[group]
        piece = lambda: w_at(start, size, lambda: q_cols(y))
        send("YR1" + group, piece, piece, lambda: at_y(y_right))
        send("YL1" + group, piece, piece, lambda: at_y(y_left))

    def y_second(group):
        start, size = GROUPS[group]
        part = size // 2
        arrived("YR1" + group, w_at(start, size, lambda: q_cols(y_left)))
        piece = lambda: w_at(start, part, lambda: q_cols(y_left))
        send("YR2" + group, piece, piece, lambda: at_y(y_right))
        w_sibling("ya", group, lambda: q_cols(y_left))
        arrived("YL1" + group, w_at(start, size, lambda: q_cols(y_right)))
        other = lambda: w_at(start + part, part, lambda: q_cols(y_right))
        send("YL2" + group, other, other, lambda: at_y(y_left))
        w_sibling("yb", group, lambda: q_cols(y_right))

    def y_third(group):
        start, size = GROUPS[group]
        part = size // 2
        arrived("YR2" + group, w_at(start, part, lambda: q_cols(y_far)))
        arrived("YL2" + group, w_at(start + part, part, lambda: q_cols(y_far)))
        w_sibling("yc", group, lambda: q_cols(y_far))

    def kv_sibling(slot):
        send("KS%d" % slot, lambda: kv_buf.at[slot, 0], lambda: kv_buf.at[slot, 1], lambda: sibling)

    def kv_from_sibling(slot):
        arrived("KS%d" % slot, kv_buf.at[slot, 1])

    def kv_step(step):
        from_left, from_right = 2 * step - 1, 2 * step
        arrived("KR%d" % step, kv_buf.at[from_left, 0])
        arrived("KL%d" % step, kv_buf.at[from_right, 0])
        if step < 3:
            send("KR%d" % (step + 1), lambda: kv_buf.at[from_left, 0], lambda: kv_buf.at[from_left + 2, 0], lambda: at_z(z_right))
            send("KL%d" % (step + 1), lambda: kv_buf.at[from_right, 0], lambda: kv_buf.at[from_right + 2, 0], lambda: at_z(z_left))
        else:
            send("KR4", lambda: kv_buf.at[5, 0, 0], lambda: kv_buf.at[7, 0, 0], lambda: at_z(z_right))
            send("KL4", lambda: kv_buf.at[6, 0, 1], lambda: kv_buf.at[7, 0, 1], lambda: at_z(z_left))
        kv_sibling(from_left)
        kv_sibling(from_right)

    def kv_last():
        arrived("KR4", kv_buf.at[7, 0, 0])
        arrived("KL4", kv_buf.at[7, 0, 1])
        kv_sibling(7)

    def local_copy(number, src, dst):
        copy = pltpu.make_async_copy(src, dst, local_sem.at[number])
        copy.start()
        return copy

    def kv_across(d, g):
        send(
            "KX%d%d" % (d, g),
            lambda: kv_hbm.at[:, :, cols(group_of(x_peers[d], g) * HD, HD)],
            lambda: kv_buf.at[0, 0, g, :, rows(x * ROWS, ROWS), :],
            lambda: at_x(x_peers[d]),
        )

    def q_across(d, g):
        send(
            "QX%d%d" % (d, g),
            lambda: q_hbm.at[:, cols(group_of(x_peers[d], g) * 768, 768)],
            lambda: q_buf.at[g, rows(x * ROWS, ROWS), :],
            lambda: at_x(x_peers[d]),
        )

    for d in (1, 3, 2):
        for g in range(2):
            kv_across(d, g)
    kv_local = [
        local_copy(g, kv_hbm.at[:, :, cols(group_of(x, g) * HD, HD)], kv_buf.at[0, 0, g, :, rows(x * ROWS, ROWS), :])
        for g in range(2)
    ]
    w_first("Q", lambda: q_cols(y))
    for d in (1, 3, 2):
        for g in range(2):
            q_across(d, g)
    q_local = [
        local_copy(2 + g, q_hbm.at[:, cols(group_of(x, g) * 768, 768)], q_buf.at[g, rows(x * ROWS, ROWS), :])
        for g in range(2)
    ]
    w_local = local_copy(4, w_hbm, w_buf.at[pl.ds(0, SHARD), :])

    for copy in kv_local:
        copy.wait()
    for d in (1, 3, 2):
        for g in range(2):
            arrived("KX%d%d" % (d, g), kv_buf.at[0, 0, g, :, rows(x_peers[4 - d] * ROWS, ROWS), :])
    send("KR1", lambda: kv_buf.at[0, 0], lambda: kv_buf.at[1, 0], lambda: at_z(z_right))
    send("KL1", lambda: kv_buf.at[0, 0], lambda: kv_buf.at[2, 0], lambda: at_z(z_left))
    kv_sibling(0)

    m_ref[...] = jnp.full(m_ref.shape, -1e30, F32)
    acc[...] = jnp.zeros(acc.shape, F32)
    chosen = (lax.broadcasted_iota(jnp.int32, (16, 64), 1) == levels_ref[span]).astype(F32).astype(BF16)
    for part in range(4):
        where = pl.ds(part * 1536, 1536)
        gate_row[:, where] = jnp.dot(chosen, gate_ref[:, where], preferred_element_type=F32)

    for copy in q_local:
        copy.wait()
    for d in (1, 3, 2):
        for g in range(2):
            arrived("QX%d%d" % (d, g), q_buf.at[g, rows(x_peers[4 - d] * ROWS, ROWS), :])
    kv_step(1)

    def prepare(tile):
        for slot in (2 * tile, 2 * tile + 1):
            step = (slot + 1) // 2
            src_z = lax.rem(z + (8 - step if slot % 2 else step), 8)
            for rel in range(2):
                src_span = (src_z // 4) * 2 + (core if rel == 0 else 1 - core)
                limit = counts_ref[src_span] * mask_ref[span, src_span]
                place = lax.broadcasted_iota(jnp.int32, (QT, HD), 0) + lax.rem(src_z, 4) * QT
                keep = jnp.where(place < limit, 1.0, 0.0).astype(BF16)
                drop = jnp.where(place < limit, 0.0, 1.0).astype(BF16)
                at = pl.ds((slot - 2 * tile) * 512 + rel * 256, QT)
                for g in range(2):
                    stand_in = jnp.broadcast_to(kv_buf[0, 0, g, 0, 0:16, :].astype(F32)[0:1], (QT, HD)).astype(BF16)
                    kp[g, at, :] = kv_buf[slot, rel, g, 0] * keep + stand_in * drop
                    ve[g, at, 0:HD] = kv_buf[slot, rel, g, 1] * keep
                    ve[g, at, HD : 2 * HD] = keep

    def a_place(g):
        d = lax.rem(2 * b + g - zl + 8, 4)
        slot = (lax.rem(d, 3) + 1) * jnp.minimum(d, 1)
        return a_buf.at[:, cols(slot * SHARD, SHARD)]

    def a_place_from(g):
        d = lax.rem(2 * (1 - b) + g - zl + 8, 4)
        slot = (lax.rem(d, 3) + 1) * jnp.minimum(d, 1)
        return a_buf.at[:, cols(slot * SHARD, SHARD)]

    partner = at_x(x + 1 - 2 * b)

    def a_out(g):
        send("A%d" % g, lambda: a_st.at[g, 1 - b], lambda: a_place(g), lambda: partner)

    def a_own(g):
        local_copy(5 + g, a_st.at[g, b], a_place(g))

    def service(i):
        todo = {
            0: lambda: (kv_from_sibling(0), kv_from_sibling(1), prepare(0)),
            1: lambda: (w_second("Q", lambda: q_cols(y)), y_first("G1"), w_sibling("q", "G1", lambda: q_cols(y))),
            2: lambda: kv_step(2),
            3: lambda: w_first("Z", z_cols),
            4: lambda: (kv_from_sibling(2), kv_from_sibling(3), prepare(1)),
            5: lambda: (w_third("Q", lambda: q_cols(y)), y_first("G2"), w_sibling("q", "G2", lambda: q_cols(y))),
            6: lambda: kv_step(3),
            8: lambda: (kv_from_sibling(4), kv_from_sibling(5), prepare(2)),
            10: lambda: kv_last(),
            11: lambda: (w_second("Z", z_cols), w_sibling("z", "G1", z_cols)),
            12: lambda: (kv_from_sibling(6), kv_from_sibling(7), prepare(3)),
            14: lambda: (w_third("Z", z_cols), w_sibling("z", "G2", z_cols)),
        }
        for when, what in todo.items():
            pl.when(i == when)(lambda what=what: (what(), None)[1])

    def attend(i, carry):
        service(i)
        g = lax.rem(i // 2, 2)
        side = lax.rem(1 - b + lax.rem(i, 2), 2)
        for j in range(3):
            h = side * 3 + j
            query = q_buf[g, :, cols(h * HD, HD)]
            scores = lax.dot_general(query, kp[g], (((1,), (1,)), ((), ())), preferred_element_type=F32)
            earlier = m_ref[g, h]
            latest = jnp.maximum(earlier, jnp.max(scores, axis=1, keepdims=True))
            weights = jnp.exp2((scores - latest[:, 0:1]) * EXP_SCALE).astype(BF16)
            factor = jnp.exp2((earlier - latest) * EXP_SCALE)
            both = jnp.dot(weights, ve[g], preferred_element_type=F32)
            m_ref[g, h] = latest
            acc[g, h, :, 0:HD] = acc[g, h, :, 0:HD] * factor + both[:, 0:HD]
            acc[g, h, :, HD : 2 * HD] = acc[g, h, :, HD : 2 * HD] * factor + both[:, HD : 2 * HD]

        @pl.when(i >= 12)
        def _():
            for j in range(3):
                h = side * 3 + j
                a_st[g, side, :, j * HD : (j + 1) * HD] = (acc[g, h, :, 0:HD] / acc[g, h, :, HD : 2 * HD]).astype(BF16)

        for when, what in {12: lambda: a_out(0), 13: lambda: a_own(0), 14: lambda: a_out(1), 15: lambda: a_own(1)}.items():
            pl.when(i == when)(what)
        return carry

    lax.fori_loop(0, 16, attend, 0)

    for g in range(2):
        pltpu.make_async_copy(a_st.at[g, b], a_place(g), local_sem.at[5 + g]).wait()
        arrived("A%d" % g, a_place_from(g))
    w_local.wait()

    order = [(0, ZC)] + [(ZC + n * QC, QC) for n in (y, y_left, y_right, y_far)]
    x_right, x_left, x_far = x_peers[1], x_peers[3], x_peers[2]

    def project(k):
        start, width = order[k]

        def piece(n, carry):
            part = jnp.dot(a_buf[...], w_buf[:, cols(start + n * 256, 256)], preferred_element_type=F32)
            o_st[k, :, cols(n * 256, 256)] = part.astype(BF16)
            return carry

        lax.fori_loop(0, width // 256, piece, 0)
        h = width // 2
        send("RA%d" % k, lambda: o_st.at[k, rows(x_far * ROWS, ROWS), pl.ds(0, h)], lambda: ra_l.at[k, :, pl.ds(0, h)], lambda: at_x(x_right))
        send("LA%d" % k, lambda: o_st.at[k, rows(x_far * ROWS, ROWS), pl.ds(h, h)], lambda: ra_r.at[k, :, pl.ds(0, h)], lambda: at_x(x_left))

    def pass_on(k):
        start, width = order[k]
        h = width // 2
        arrived("RA%d" % k, ra_l.at[k, :, pl.ds(0, h)])
        mine = o_st[k, rows(x_right * ROWS, ROWS), 0:h].astype(F32)
        o_st[k, rows(x_right * ROWS, ROWS), 0:h] = (mine + ra_l[k, :, 0:h].astype(F32)).astype(BF16)
        send("RB%d" % k, lambda: o_st.at[k, rows(x_right * ROWS, ROWS), pl.ds(0, width)], lambda: rb_l.at[k, :, pl.ds(0, width)], lambda: at_x(x_right))
        arrived("LA%d" % k, ra_r.at[k, :, pl.ds(0, h)])
        mine = o_st[k, rows(x_left * ROWS, ROWS), h:width].astype(F32)
        o_st[k, rows(x_left * ROWS, ROWS), h:width] = (mine + ra_r[k, :, 0:h].astype(F32)).astype(BF16)
        send("LB%d" % k, lambda: o_st.at[k, rows(x_left * ROWS, ROWS), pl.ds(0, width)], lambda: rb_r.at[k, :, pl.ds(0, width)], lambda: at_x(x_left))

    def finish(k):
        start, width = order[k]
        arrived("RB%d" % k, rb_l.at[k, :, pl.ds(0, width)])
        arrived("LB%d" % k, rb_r.at[k, :, pl.ds(0, width)])
        total = o_st[k, rows(x * ROWS, ROWS), 0:width].astype(F32)
        total = total + rb_l[k, :, 0:width].astype(F32) + rb_r[k, :, 0:width].astype(F32)
        place = lax.broadcasted_iota(jnp.int32, (ROWS, width), 0) + head * ROWS
        gated = total * gate_row[0:1, cols(start, width)]
        out_ref[:, cols(start, width)] = jnp.where(place < counts_ref[span], gated, 0.0).astype(BF16)

    w_from_sibling("z", "G1", z_cols_sib)
    w_from_sibling("z", "G2", z_cols_sib)
    project(0)
    w_from_sibling("q", "G1", lambda: q_cols_sib(y))
    w_from_sibling("q", "G2", lambda: q_cols_sib(y))
    project(1)
    y_second("G1")
    pass_on(0)
    y_second("G2")
    pass_on(1)
    for group in GROUPS:
        w_from_sibling("ya", group, lambda: q_cols_sib(y_left))
    project(2)
    for group in GROUPS:
        w_from_sibling("yb", group, lambda: q_cols_sib(y_right))
    project(3)
    finish(0)
    pass_on(2)
    pass_on(3)
    y_third("G1")
    y_third("G2")
    for group in GROUPS:
        w_from_sibling("yc", group, lambda: q_cols_sib(y_far))
    project(4)
    finish(1)
    finish(2)
    pass_on(4)
    finish(3)
    finish(4)
    for name, src, dst, where in sent:
        message(name, src(), dst(), where()).wait_send()


def local(queries, key_value, w_out, gate_table, levels, span_mask, counts):
    kv = jnp.transpose(key_value, (1, 0, 2))
    anywhere = pl.BlockSpec(memory_space=pl.ANY)
    vmem = pl.BlockSpec(memory_space=pltpu.VMEM)
    smem = pl.BlockSpec(memory_space=pltpu.SMEM)
    return pl.pallas_call(
        kernel,
        out_shape=jax.ShapeDtypeStruct((ROWS, D), BF16),
        in_specs=[anywhere, anywhere, anywhere, vmem, smem, smem, smem],
        out_specs=vmem,
        scratch_shapes=[
            pltpu.VMEM((2, QT, 768), BF16),
            pltpu.VMEM((8, 2, 2, 2, QT, HD), BF16),
            pltpu.VMEM((2, 1024, HD), BF16),
            pltpu.VMEM((2, 1024, 2 * HD), BF16),
            pltpu.VMEM((2, 6, QT, HD), F32),
            pltpu.VMEM((2, 6, QT, 2 * HD), F32),
            pltpu.VMEM((2, 2, QT, SHARD), BF16),
            pltpu.VMEM((QT, 4 * SHARD), BF16),
            pltpu.VMEM((4 * SHARD, D), BF16),
            pltpu.VMEM((5, QT, QC), BF16),
            pltpu.VMEM((5, ROWS, QC // 2), BF16),
            pltpu.VMEM((5, ROWS, QC // 2), BF16),
            pltpu.VMEM((5, ROWS, QC), BF16),
            pltpu.VMEM((5, ROWS, QC), BF16),
            pltpu.VMEM((16, D), F32),
            pltpu.SemaphoreType.DMA((N_MESSAGES,)),
            pltpu.SemaphoreType.DMA((N_MESSAGES,)),
            pltpu.SemaphoreType.DMA((N_LOCAL,)),
        ],
        compiler_params=pltpu.CompilerParams(
            collective_id=0, has_side_effects=True, vmem_limit_bytes=56 * 1024 * 1024
        ),
    )(queries, kv, w_out, gate_table, levels, span_mask, counts)


def solution(mesh):
    in_specs = (
        P(("rep", "span", "head"), None),
        P(("rep", "span", "head"), None, None),
        P("head", None),
        P(),
        P("rep"),
        P("rep", None),
        P("rep"),
    )
    out_specs = P(("rep", "span", "head"), None)
    return jax.shard_map(local, mesh=mesh, in_specs=in_specs, out_specs=out_specs, check_vma=False)
```

time: 391 us -> 113 us (0.29)
  waiting for transfers between devices: 194 us -> 0 us
  Pallas kernels: 0 us -> 109 us
  other arithmetic: 78.1 us -> 0 us
  local copies, waits for them, and re-layouts: 47.1 us -> 3.77 us
  matrix products: 40.2 us -> 0 us
  starting transfers between devices: 15.4 us -> 0 us
  between operations: 13.7 us -> 0.01 us
    reduce_scatter x1 -> x0, waiting for transfers between devices: 149 us -> none  [local(): lax.psum_scatter(jnp.dot(attended, w_out, preferred_element_type=jnp.floa...]
    pallas_call x0 -> x1, Pallas kernels: none -> 109 us  [local(): pl.pallas_call(kernel, out_shape=jax.ShapeDtypeStruct((ROWS, D), BF16), i...]
    all_to_all x2 -> x0, waiting for transfers between devices: 44.3 us -> none  [the longest x1 30.6 us: local(): lax.all_to_all(spread.reshape(row_total, 2, KV_GROUPS * copies * HD), 'he...]
    dot_general x26 -> x0, matrix products: 40.2 us -> none  [the longest x12 18.4 us: one_head(): jnp.dot(weights.astype(jnp.bfloat16), value_rows, preferred_element_type=...]
    unnamed x1 -> x0, other arithmetic: 34.3 us -> none
    another operation x36 -> x0, other arithmetic: 24.9 us -> none
    all_to_all x2 -> x0, starting transfers between devices: 15.2 us -> none  [the longest x1 9.01 us: local(): lax.all_to_all(query_rows, 'head', split_axis=2, concat_axis=0, tiled=True)]
    reduce_sum x16 -> x0, other arithmetic: 14.2 us -> none  [the longest x12 12.7 us: one_head(): new_total = earlier_total * factor + jnp.sum(weights, axis=1)]
  transfers between devices with their start and end apart: 4 -> 0, of which waited for: 3 -> 0; matrix products, arithmetic and copies ran while one was open for 16% -> 0% of each run, Pallas kernels for 0% -> 0%
where the time goes in v1:
time: 113 us
  Pallas kernels  109 us (96%)
  local copies, waits for them, and re-layouts  3.77 us (3%)
    pallas_call x1, Pallas kernels, local(): pl.pallas_call(kernel, out_shape=jax.ShapeDtypeStruct((ROWS, D), BF16), i...  109 us
    unnamed x2, local copies, waits for them, and re-layouts  3.77 us

profile of v1, /device:TPU:1, one launch (start us, length us, event | category | flops | bytes accessed | tf_op | source)
XLA Modules:
  0.0 113.0 jit_solution(310084505703263248)
XLA Ops:
  0.0 1.7 %copy.10 = bf16[64,2,1024]{2,0,1:T(8,128)(2,1)} copy(bf16[64,2,1024]{2,1,0:T(2,128)(2,1)} %param.8) | data formatting | bytes 524288 | tf_op args[1]
  1.7 109.3 %shard_map.73 = bf16[64,6144]{1,0:T(8,128)(2,1)} custom-call(bf16[64,6144]{1,0:T(8,128)(2,1)} %q_hbm.1, bf16[2,64,1024]{2,1,0:T(8,128)(2,1)} %bitcast.3, bf16[384,6144]{1,0:T(8,128)(2,1)} %w_hbm.1, bf16[64,6144]{1,0:T(8,128)(2,1)} %gate_ref.1, s32[4]{0:T(128)} %levels_ref.1, s32[4,4]{1,0:T(4,128)} %mask_ref.1, s32[4]{0:T(128)} %counts_ref.1), custom_call_target="tpu_custom_call" | custom-call | tf_op jit(solution)/shard_map/pallas_call | solution.py:411
  111.0 2.1 %copy.12 = bf16[64,6144]{1,0:T(8,128)(2,1)} copy(bf16[64,6144]{1,0:T(8,128)(2,1)} %shard_map.73) | data formatting | bytes 1572864

commit v2 on v1

v2 whole, which is shorter than its diff:
```python
import jax
import jax.numpy as jnp
from jax import lax
from jax.experimental import pallas as pl
from jax.experimental.pallas import tpu as pltpu
from jax.sharding import PartitionSpec as P

MESH = pl.DeviceIdType.MESH
HD = 128
SPAN = 1024
D = 6144
ROWS = 64
QT = 256
SHARD = 384
NC = 3072
QC = 768
EXP_SCALE = HD**-0.5 * 1.4426950408889634
F32 = jnp.float32
BF16 = jnp.bfloat16


class Names:
    def __init__(self):
        self.ids = {}

    def __call__(self, name):
        return self.ids.setdefault(name, len(self.ids))


N_MESSAGES = 130
N_LOCAL = 8


def kernel(
    q_hbm, kv_hbm, w_hbm, gate_ref, levels_ref, mask_ref, counts_ref, out_ref,
    q_buf, kv_buf, kp, ve, m_ref, acc, a_st, a_buf, w_buf, o_st, ra_l, ra_r, rb_l, rb_r,
    f_out, f_in, gate_row, send_sem, recv_sem, local_sem,
):
    span = lax.axis_index("span")
    head = lax.axis_index("head")
    y = lax.axis_index("rep")
    core = lax.rem(span, 2)
    zl = head // 4
    x = lax.rem(head, 4)
    z = (span // 2) * 4 + zl
    a = x // 2
    b = lax.rem(x, 2)

    def at_x(xx):
        return {"head": zl * 4 + xx}

    def at_z(zz):
        return {"span": (zz // 4) * 2 + core, "head": lax.rem(zz, 4) * 4 + x}

    def at_y(yy):
        return {"rep": yy}

    sibling = {"span": (span // 2) * 2 + 1 - core}
    x_peers = [lax.rem(x + d, 4) for d in range(4)]
    z_right, z_left = lax.rem(z + 1, 8), lax.rem(z + 7, 8)
    y_right, y_left = lax.rem(y + 1, 4), lax.rem(y + 3, 4)
    y_far = lax.rem(y + 2, 4)
    z_right2, z_left2 = lax.rem(z + 2, 8), lax.rem(z + 6, 8)
    parity = lax.rem(z, 2)
    z_pair = z + 1 - 2 * parity

    names = Names()
    sent = []

    def message(name, src, dst, where):
        number = names(name)
        return pltpu.make_async_remote_copy(
            src_ref=src, dst_ref=dst, send_sem=send_sem.at[number], recv_sem=recv_sem.at[number],
            device_id=where, device_id_type=MESH,
        )

    def send(name, src, dst, where):
        message(name, src(), dst(), where()).start()
        sent.append((name, src, dst, where))

    def arrived(name, dst):
        message(name, dst, dst, sibling).wait_recv()

    barrier = pltpu.get_barrier_semaphore()
    peers = [at_x(x_peers[d]) for d in (1, 2, 3)]
    peers += [at_z(zz) for zz in (z_right, z_left, z_right2, z_left2)]
    peers += [at_y(yy) for yy in (y_right, y_left, y_far)]
    peers += [sibling]
    for peer in peers:
        pl.semaphore_signal(barrier, inc=1, device_id=peer, device_id_type=MESH)
    pl.semaphore_wait(barrier, len(peers))

    def group_of(xx, g):
        return 4 * lax.rem(xx, 2) + 2 * g + xx // 2

    def cols(start, width):
        return pl.ds(pl.multiple_of(start, 128), width)

    def rows(start, width):
        return pl.ds(pl.multiple_of(start, 64), width)

    half = SHARD // 2
    WIDE = QC // 2

    def q_cols(n, of_core=None):
        return cols(n * QC + (core if of_core is None else of_core) * WIDE, WIDE)

    def w_own(start, size, side):
        return w_hbm.at[pl.ds(start, size), cols(side * NC + y * QC + core * WIDE, WIDE)]

    def w_at(start, size, n, of_core=None):
        return w_buf.at[pl.ds(start, size), q_cols(n, of_core)]

    def w_near():
        send("WR1", lambda: w_own(0, SHARD, 1 - parity), lambda: w_at(SHARD, SHARD, y), lambda: at_z(z_right))
        send("WL1", lambda: w_own(0, SHARD, 1 - parity), lambda: w_at(2 * SHARD, SHARD, y), lambda: at_z(z_left))

    def w_far():
        send("WR2", lambda: w_own(0, half, parity), lambda: w_at(3 * SHARD, half, y), lambda: at_z(z_right2))
        send("WL2", lambda: w_own(half, half, parity), lambda: w_at(3 * SHARD + half, half, y), lambda: at_z(z_left2))

    def y_out(slot):
        send("YR%d" % slot, lambda: w_at(slot * SHARD, SHARD, y), lambda: w_at(slot * SHARD, SHARD, y), lambda: at_y(y_right))
        send("YL%d" % slot, lambda: w_at(slot * SHARD, SHARD, y), lambda: w_at(slot * SHARD, SHARD, y), lambda: at_y(y_left))
        send("YF%d" % slot, lambda: w_at(slot * SHARD, SHARD, y), lambda: w_at(slot * SHARD, SHARD, y), lambda: at_y(y_far))

    def w_got_near():
        arrived("WR1", w_at(SHARD, SHARD, y))
        y_out(1)
        arrived("WL1", w_at(2 * SHARD, SHARD, y))
        y_out(2)

    def w_sibling(name, n):
        send("S" + name, lambda: w_at(SHARD, 3 * SHARD, n), lambda: w_at(SHARD, 3 * SHARD, n), lambda: sibling)

    def w_from_sibling(name, n):
        arrived("S" + name, w_at(SHARD, 3 * SHARD, n, 1 - core))

    def w_got_far():
        arrived("WR2", w_at(3 * SHARD, half, y))
        arrived("WL2", w_at(3 * SHARD + half, half, y))
        y_out(3)
        w_sibling("YO", y)

    def y_got(way, n):
        for slot in (1, 2, 3):
            arrived("%s%d" % (way, slot), w_at(slot * SHARD, SHARD, n))
        w_sibling(way, n)

    def kv_sibling(slot, g):
        send("KS%d%d" % (slot, g), lambda: kv_buf.at[slot, 0, g], lambda: kv_buf.at[slot, 1, g], lambda: sibling)

    def kv_from_sibling(slot, g):
        arrived("KS%d%d" % (slot, g), kv_buf.at[slot, 1, g])

    def kv_send(step, from_slot, g, right):
        to_slot = 2 * step - 1 if right else 2 * step
        if step == 4:
            to_slot = 7
        send(
            ("KR%d%d" if right else "KL%d%d") % (step, g),
            lambda: kv_buf.at[from_slot, 0, g],
            lambda: kv_buf.at[to_slot, 0, g],
            lambda: at_z(z_right if right else z_left),
        )

    def kv_step(step, g):
        from_left, from_right = 2 * step - 1, 2 * step
        arrived("KR%d%d" % (step, g), kv_buf.at[from_left, 0, g])
        if step < 3 or g == 0:
            kv_send(step + 1, from_left, g, True)
        arrived("KL%d%d" % (step, g), kv_buf.at[from_right, 0, g])
        if step < 3 or g == 1:
            kv_send(step + 1, from_right, g, False)
        kv_sibling(from_left, g)
        kv_sibling(from_right, g)

    def kv_last():
        arrived("KR40", kv_buf.at[7, 0, 0])
        kv_sibling(7, 0)
        arrived("KL41", kv_buf.at[7, 0, 1])
        kv_sibling(7, 1)

    def local_copy(number, src, dst):
        copy = pltpu.make_async_copy(src, dst, local_sem.at[number])
        copy.start()
        return copy

    def kv_across(d, g):
        send(
            "KX%d%d" % (d, g),
            lambda: kv_hbm.at[:, :, cols(group_of(x_peers[d], g) * HD, HD)],
            lambda: kv_buf.at[0, 0, g, :, rows(x * ROWS, ROWS), :],
            lambda: at_x(x_peers[d]),
        )

    def q_across(d, g):
        send(
            "QX%d%d" % (d, g),
            lambda: q_hbm.at[:, cols(group_of(x_peers[d], g) * 768, 768)],
            lambda: q_buf.at[g, rows(x * ROWS, ROWS), :],
            lambda: at_x(x_peers[d]),
        )

    for g in range(2):
        for d in (1, 3, 2):
            kv_across(d, g)
    kv_local = [
        local_copy(g, kv_hbm.at[:, :, cols(group_of(x, g) * HD, HD)], kv_buf.at[0, 0, g, :, rows(x * ROWS, ROWS), :])
        for g in range(2)
    ]
    w_near()
    for d in (1, 3, 2):
        for g in range(2):
            q_across(d, g)
    q_local = [
        local_copy(2 + g, q_hbm.at[:, cols(group_of(x, g) * 768, 768)], q_buf.at[g, rows(x * ROWS, ROWS), :])
        for g in range(2)
    ]
    w_local = local_copy(4, w_hbm.at[:, cols(parity * NC, NC)], w_buf.at[pl.ds(0, SHARD), :])

    m_ref[...] = jnp.full(m_ref.shape, -1e30, F32)
    acc[...] = jnp.zeros(acc.shape, F32)

    for g in range(2):
        kv_local[g].wait()
        for d in (1, 3, 2):
            arrived("KX%d%d" % (d, g), kv_buf.at[0, 0, g, :, rows(x_peers[4 - d] * ROWS, ROWS), :])
        kv_send(1, 0, g, True)
        kv_send(1, 0, g, False)
        kv_sibling(0, g)

    chosen = (lax.broadcasted_iota(jnp.int32, (16, 64), 1) == levels_ref[span]).astype(F32).astype(BF16)
    for part in range(2):
        gate_row[:, part * 1536 : (part + 1) * 1536] = jnp.dot(
            chosen, gate_ref[:, cols(parity * NC + part * 1536, 1536)], preferred_element_type=F32
        )

    kv_step(1, 0)
    w_got_near()
    kv_step(1, 1)
    for copy in q_local:
        copy.wait()
    for d in (1, 3, 2):
        for g in range(2):
            arrived("QX%d%d" % (d, g), q_buf.at[g, rows(x_peers[4 - d] * ROWS, ROWS), :])

    def prepare(tile, g):
        for slot in (2 * tile, 2 * tile + 1):
            kv_from_sibling(slot, g)
        for slot in (2 * tile, 2 * tile + 1):
            step = (slot + 1) // 2
            src_z = lax.rem(z + (8 - step if slot % 2 else step), 8)
            for rel in range(2):
                src_span = (src_z // 4) * 2 + (core if rel == 0 else 1 - core)
                limit = counts_ref[src_span] * mask_ref[span, src_span]
                place = lax.broadcasted_iota(jnp.int32, (QT, HD), 0) + lax.rem(src_z, 4) * QT
                keep = jnp.where(place < limit, 1.0, 0.0).astype(BF16)
                drop = jnp.where(place < limit, 0.0, 1.0).astype(BF16)
                at = pl.ds((slot - 2 * tile) * 512 + rel * 256, QT)
                stand_in = jnp.broadcast_to(kv_buf[0, 0, g, 0, 0:16, :].astype(F32)[0:1], (QT, HD)).astype(BF16)
                kp[g, at, :] = kv_buf[slot, rel, g, 0] * keep + stand_in * drop
                ve[g, at, 0:HD] = kv_buf[slot, rel, g, 1] * keep
                ve[g, at, HD : 2 * HD] = keep

    def a_place(place, shard, zz):
        d = lax.rem(shard - lax.rem(zz, 4) + 4, 4)
        slot = (lax.rem(d, 3) + 1) * jnp.minimum(d, 1)
        return a_buf.at[pl.ds(place * QT, QT), cols(slot * SHARD, SHARD)]

    partner = at_x(x + 1 - 2 * b)

    def a_across(g):
        send("AX%d" % g, lambda: a_st.at[g, 1 - b], lambda: a_place(0, 2 * b + g, z), lambda: partner)

    def a_own(g):
        local_copy(5 + g, a_st.at[g, b], a_place(0, 2 * b + g, z))
        send("AZ%d" % g, lambda: a_st.at[g, b], lambda: a_place(1, 2 * b + g, z_pair), lambda: at_z(z_pair))

    def a_forward(g):
        mine = lambda: a_place(0, 2 * (1 - b) + g, z)
        arrived("AX%d" % g, mine())
        send("AF%d" % g, mine, lambda: a_place(1, 2 * (1 - b) + g, z_pair), lambda: at_z(z_pair))

    def service(i):
        todo = {
            0: lambda: prepare(0, 0),
            1: lambda: prepare(0, 1),
            2: lambda: kv_step(2, 0),
            3: lambda: kv_step(2, 1),
            4: lambda: prepare(1, 0),
            5: lambda: prepare(1, 1),
            6: lambda: kv_step(3, 0),
            7: lambda: kv_step(3, 1),
            8: lambda: (prepare(2, 0), w_far()),
            9: lambda: prepare(2, 1),
            10: lambda: kv_last(),
            12: lambda: prepare(3, 0),
            13: lambda: prepare(3, 1),
            14: lambda: w_got_far(),
        }
        for when, what in todo.items():
            pl.when(i == when)(lambda what=what: (what(), None)[1])

    def attend(i, carry):
        service(i)
        g = lax.rem(i, 2)
        side = lax.rem(1 - b + lax.rem(i // 2, 2), 2)
        heads = [side * 3 + j for j in range(3)]
        keys, values = kp[g], ve[g]
        queries = [q_buf[g, :, cols(h * HD, HD)] for h in heads]
        earlier = [m_ref[g, h] for h in heads]
        sums = [acc[g, h] for h in heads]
        latest, results = [], []

        def score(j):
            return lax.dot_general(queries[j], keys, (((1,), (1,)), ((), ())), preferred_element_type=F32)

        ahead = score(0)
        for j in range(3):
            scores = ahead
            if j < 2:
                ahead = score(j + 1)
            top = jnp.maximum(earlier[j], jnp.max(scores, axis=1, keepdims=True))
            latest.append(top)
            weights = jnp.exp2((scores - jnp.concatenate([top] * 8, axis=1)) * EXP_SCALE).astype(BF16)
            factor = jnp.exp2((earlier[j] - top) * EXP_SCALE)
            both = jnp.dot(weights, values, preferred_element_type=F32)
            results.append(sums[j] * jnp.concatenate([factor] * 2, axis=1) + both)
        for j in range(3):
            m_ref[g, heads[j]] = latest[j]
            acc[g, heads[j]] = results[j]

        @pl.when(i >= 12)
        def _():
            for j in range(3):
                h = side * 3 + j
                a_st[g, side, :, j * HD : (j + 1) * HD] = (acc[g, h, :, 0:HD] / acc[g, h, :, HD : 2 * HD]).astype(BF16)

        for when, what in {12: lambda: a_across(0), 13: lambda: a_across(1), 14: lambda: a_own(0), 15: lambda: a_own(1)}.items():
            pl.when(i == when)(what)
        return carry

    lax.fori_loop(0, 16, attend, 0)

    for g in range(2):
        a_forward(g)
    for g in range(2):
        pltpu.make_async_copy(a_st.at[g, b], a_place(0, 2 * b + g, z), local_sem.at[5 + g]).wait()
    w_local.wait()

    quarters = [y, y_left, y_right, y_far]
    x_right, x_left, x_far = x_peers[1], x_peers[3], x_peers[2]
    width = QC

    def project(k):
        tokens = pl.ds((k // 4) * QT, QT)
        start = quarters[k % 4] * QC

        def piece(n, carry):
            part = jnp.dot(a_buf[tokens, :], w_buf[:, cols(start + n * 256, 256)], preferred_element_type=F32)
            o_st[k, :, cols(n * 256, 256)] = part.astype(BF16)
            return carry

        lax.fori_loop(0, width // 256, piece, 0)
        h = width // 2
        send("RA%d" % k, lambda: o_st.at[k, rows(x_far * ROWS, ROWS), pl.ds(0, h)], lambda: ra_l.at[k, :, pl.ds(0, h)], lambda: at_x(x_right))
        send("LA%d" % k, lambda: o_st.at[k, rows(x_far * ROWS, ROWS), pl.ds(h, h)], lambda: ra_r.at[k, :, pl.ds(0, h)], lambda: at_x(x_left))

    def pass_on(k):
        h = width // 2
        arrived("RA%d" % k, ra_l.at[k, :, pl.ds(0, h)])
        mine = o_st[k, rows(x_right * ROWS, ROWS), 0:h].astype(F32)
        o_st[k, rows(x_right * ROWS, ROWS), 0:h] = (mine + ra_l[k, :, 0:h].astype(F32)).astype(BF16)
        send("RB%d" % k, lambda: o_st.at[k, rows(x_right * ROWS, ROWS), pl.ds(0, width)], lambda: rb_l.at[k, :, pl.ds(0, width)], lambda: at_x(x_right))
        arrived("LA%d" % k, ra_r.at[k, :, pl.ds(0, h)])
        mine = o_st[k, rows(x_left * ROWS, ROWS), h:width].astype(F32)
        o_st[k, rows(x_left * ROWS, ROWS), h:width] = (mine + ra_r[k, :, 0:h].astype(F32)).astype(BF16)
        send("LB%d" % k, lambda: o_st.at[k, rows(x_left * ROWS, ROWS), pl.ds(0, width)], lambda: rb_r.at[k, :, pl.ds(0, width)], lambda: at_x(x_left))

    def finish(k):
        arrived("RB%d" % k, rb_l.at[k, :, pl.ds(0, width)])
        arrived("LB%d" % k, rb_r.at[k, :, pl.ds(0, width)])
        total = o_st[k, rows(x * ROWS, ROWS), 0:width].astype(F32)
        total = total + rb_l[k, :, 0:width].astype(F32) + rb_r[k, :, 0:width].astype(F32)
        n = quarters[k % 4]
        owner = head if k < 4 else lax.rem(z_pair, 4) * 4 + x
        place = lax.broadcasted_iota(jnp.int32, (ROWS, width), 0) + owner * ROWS
        gated = total * gate_row[0:1, cols(n * QC, QC)]
        result = jnp.where(place < counts_ref[span], gated, 0.0).astype(BF16)
        if k < 4:
            out_ref[:, cols(parity * NC + n * QC, QC)] = result
        else:
            f_out[k - 4] = result
            send("F%d" % (k - 4), lambda: f_out.at[k - 4], lambda: f_in.at[k - 4], lambda: at_z(z_pair))

    def take(k):
        arrived("F%d" % k, f_in.at[k])
        out_ref[:, cols((1 - parity) * NC + quarters[k] * QC, QC)] = f_in[k]

    w_from_sibling("YO", y)
    project(0)
    y_got("YR", y_left)
    y_got("YL", y_right)
    y_got("YF", y_far)
    w_from_sibling("YR", y_left)
    project(1)
    w_from_sibling("YL", y_right)
    project(2)
    pass_on(0)
    w_from_sibling("YF", y_far)
    pass_on(1)
    pass_on(2)
    for g in range(2):
        arrived("AZ%d" % g, a_place(1, 2 * b + g, z))
        arrived("AF%d" % g, a_place(1, 2 * (1 - b) + g, z))
    for k in (4, 5, 6, 7):
        project(k)
    pass_on(4)
    project(3)
    finish(0)
    pass_on(5)
    finish(1)
    pass_on(6)
    finish(2)
    pass_on(7)
    pass_on(3)
    for k in (4, 5, 6, 7):
        finish(k)
    for k in range(4):
        take(k)
    finish(3)
    for name, src, dst, where in sent:
        message(name, src(), dst(), where()).wait_send()


def local(queries, key_value, w_out, gate_table, levels, span_mask, counts):
    kv = jnp.transpose(key_value, (1, 0, 2))
    anywhere = pl.BlockSpec(memory_space=pl.ANY)
    vmem = pl.BlockSpec(memory_space=pltpu.VMEM)
    smem = pl.BlockSpec(memory_space=pltpu.SMEM)
    return pl.pallas_call(
        kernel,
        out_shape=jax.ShapeDtypeStruct((ROWS, D), BF16),
        in_specs=[anywhere, anywhere, anywhere, vmem, smem, smem, smem],
        out_specs=vmem,
        scratch_shapes=[
            pltpu.VMEM((2, QT, 768), BF16),
            pltpu.VMEM((8, 2, 2, 2, QT, HD), BF16),
            pltpu.VMEM((2, 1024, HD), BF16),
            pltpu.VMEM((2, 1024, 2 * HD), BF16),
            pltpu.VMEM((2, 6, QT, HD), F32),
            pltpu.VMEM((2, 6, QT, 2 * HD), F32),
            pltpu.VMEM((2, 2, QT, SHARD), BF16),
            pltpu.VMEM((2 * QT, 4 * SHARD), BF16),
            pltpu.VMEM((4 * SHARD, NC), BF16),
            pltpu.VMEM((8, QT, QC), BF16),
            pltpu.VMEM((8, ROWS, QC // 2), BF16),
            pltpu.VMEM((8, ROWS, QC // 2), BF16),
            pltpu.VMEM((8, ROWS, QC), BF16),
            pltpu.VMEM((8, ROWS, QC), BF16),
            pltpu.VMEM((4, ROWS, QC), BF16),
            pltpu.VMEM((4, ROWS, QC), BF16),
            pltpu.VMEM((16, NC), F32),
            pltpu.SemaphoreType.DMA((N_MESSAGES,)),
            pltpu.SemaphoreType.DMA((N_MESSAGES,)),
            pltpu.SemaphoreType.DMA((N_LOCAL,)),
        ],
        compiler_params=pltpu.CompilerParams(
            collective_id=0, has_side_effects=True, vmem_limit_bytes=56 * 1024 * 1024
        ),
    )(queries, kv, w_out, gate_table, levels, span_mask, counts)


def solution(mesh):
    in_specs = (
        P(("rep", "span", "head"), None),
        P(("rep", "span", "head"), None, None),
        P("head", None),
        P(),
        P("rep"),
        P("rep", None),
        P("rep"),
    )
    out_specs = P(("rep", "span", "head"), None)
    return jax.shard_map(local, mesh=mesh, in_specs=in_specs, out_specs=out_specs, check_vma=False)
```

time: 113 us -> 98.4 us (0.87)
  Pallas kernels: 109 us -> 93.6 us
    pallas_call x1, Pallas kernels: 109 us -> 93.6 us  [local(): pl.pallas_call(kernel, out_shape=jax.ShapeDtypeStruct((ROWS, D), BF16), i...]
where the time goes in v2:
time: 98.4 us; the launch traced here: 97.4 us
  Pallas kernels  93.6 us (95%)
  local copies, waits for them, and re-layouts  3.77 us (4%)
    pallas_call x1, Pallas kernels, local(): pl.pallas_call(kernel, out_shape=jax.ShapeDtypeStruct((ROWS, D), BF16), i...  93.6 us
    unnamed x2, local copies, waits for them, and re-layouts  3.77 us

profile of v2, /device:TPU:1, one launch (start us, length us, event | category | flops | bytes accessed | tf_op | source)
XLA Modules:
  0.0 97.4 jit_solution(13918382383605879303)
XLA Ops:
  0.0 1.7 %copy.10 = bf16[64,2,1024]{2,0,1:T(8,128)(2,1)} copy(bf16[64,2,1024]{2,1,0:T(2,128)(2,1)} %param.8) | data formatting | bytes 524288 | tf_op args[1]
  1.7 93.6 %shard_map.73 = bf16[64,6144]{1,0:T(8,128)(2,1)} custom-call(bf16[64,6144]{1,0:T(8,128)(2,1)} %q_hbm.1, bf16[2,64,1024]{2,1,0:T(8,128)(2,1)} %bitcast.3, bf16[384,6144]{1,0:T(8,128)(2,1)} %w_hbm.1, bf16[64,6144]{1,0:T(8,128)(2,1)} %gate_ref.1, s32[4]{0:T(128)} %levels_ref.1, s32[4,4]{1,0:T(4,128)} %mask_ref.1, s32[4]{0:T(128)} %counts_ref.1), custom_call_target="tpu_custom_call" | custom-call | tf_op jit(solution)/shard_map/pallas_call | solution.py:442
  95.3 2.1 %copy.12 = bf16[64,6144]{1,0:T(8,128)(2,1)} copy(bf16[64,6144]{1,0:T(8,128)(2,1)} %shard_map.73) | data formatting | bytes 1572864

commit v3 on v2

--- a/solution.py
+++ b/solution.py
@@ -32,8 +32,8 @@
 
 
 def kernel(
-    q_hbm, kv_hbm, w_hbm, gate_ref, levels_ref, mask_ref, counts_ref, out_ref,
-    q_buf, kv_buf, kp, ve, m_ref, acc, a_st, a_buf, w_buf, o_st, ra_l, ra_r, rb_l, rb_r,
+    q_hbm, kv_ref, w_hbm, gate_ref, levels_ref, mask_ref, counts_ref, out_ref,
+    kv_st, q_buf, kv_buf, kp, ve, m_ref, acc, a_st, a_buf, w_buf, o_st, ra_l, ra_r, rb_l, rb_r,
     f_out, f_in, gate_row, send_sem, recv_sem, local_sem,
 ):
     span = lax.axis_index("span")
@@ -78,6 +78,13 @@
         message(name, src(), dst(), where()).start()
         sent.append((name, src, dst, where))
 
+    def drain(*kinds):
+        for item in list(sent):
+            if item[0].startswith(kinds):
+                name, src, dst, where = item
+                message(name, src(), dst(), where()).wait_send()
+                sent.remove(item)
+
     def arrived(name, dst):
         message(name, dst, dst, sibling).wait_recv()
 
@@ -88,6 +95,10 @@
     peers += [sibling]
     for peer in peers:
         pl.semaphore_signal(barrier, inc=1, device_id=peer, device_id_type=MESH)
+    kv_st[0] = kv_ref[:, 0, :]
+    kv_st[1] = kv_ref[:, 1, :]
+    m_ref[...] = jnp.full(m_ref.shape, -1e30, F32)
+    acc[...] = jnp.zeros(acc.shape, F32)
     pl.semaphore_wait(barrier, len(peers))
 
     def group_of(xx, g):
@@ -189,38 +200,47 @@
     def kv_across(d, g):
         send(
             "KX%d%d" % (d, g),
-            lambda: kv_hbm.at[:, :, cols(group_of(x_peers[d], g) * HD, HD)],
+            lambda: kv_st.at[:, :, cols(group_of(x_peers[d], g) * HD, HD)],
             lambda: kv_buf.at[0, 0, g, :, rows(x * ROWS, ROWS), :],
             lambda: at_x(x_peers[d]),
         )
 
-    def q_across(d, g):
+    def q_side(xx, turn):
+        return lax.rem(1 - lax.rem(xx, 2) + turn, 2)
+
+    def q_across(d, g, turn):
+        start = lambda: group_of(x_peers[d], g) * 768 + q_side(x_peers[d], turn) * SHARD
         send(
-            "QX%d%d" % (d, g),
-            lambda: q_hbm.at[:, cols(group_of(x_peers[d], g) * 768, 768)],
-            lambda: q_buf.at[g, rows(x * ROWS, ROWS), :],
+            "QX%d%d%d" % (d, g, turn),
+            lambda: q_hbm.at[:, cols(start(), SHARD)],
+            lambda: q_buf.at[g, rows(x * ROWS, ROWS), cols(q_side(x_peers[d], turn) * SHARD, SHARD)],
             lambda: at_x(x_peers[d]),
         )
+
+    def q_wait(g, turn):
+        for d in (1, 3, 2):
+            arrived(
+                "QX%d%d%d" % (d, g, turn),
+                q_buf.at[g, rows(x_peers[4 - d] * ROWS, ROWS), cols(q_side(x, turn) * SHARD, SHARD)],
+            )
 
     for g in range(2):
         for d in (1, 3, 2):
             kv_across(d, g)
     kv_local = [
-        local_copy(g, kv_hbm.at[:, :, cols(group_of(x, g) * HD, HD)], kv_buf.at[0, 0, g, :, rows(x * ROWS, ROWS), :])
+        local_copy(g, kv_st.at[:, :, cols(group_of(x, g) * HD, HD)], kv_buf.at[0, 0, g, :, rows(x * ROWS, ROWS), :])
         for g in range(2)
     ]
     w_near()
-    for d in (1, 3, 2):
+    for turn in range(2):
         for g in range(2):
-            q_across(d, g)
+            for d in (1, 3, 2):
+                q_across(d, g, turn)
     q_local = [
         local_copy(2 + g, q_hbm.at[:, cols(group_of(x, g) * 768, 768)], q_buf.at[g, rows(x * ROWS, ROWS), :])
         for g in range(2)
     ]
     w_local = local_copy(4, w_hbm.at[:, cols(parity * NC, NC)], w_buf.at[pl.ds(0, SHARD), :])
-
-    m_ref[...] = jnp.full(m_ref.shape, -1e30, F32)
-    acc[...] = jnp.zeros(acc.shape, F32)
 
     for g in range(2):
         kv_local[g].wait()
@@ -230,21 +250,11 @@
         kv_send(1, 0, g, False)
         kv_sibling(0, g)
 
-    chosen = (lax.broadcasted_iota(jnp.int32, (16, 64), 1) == levels_ref[span]).astype(F32).astype(BF16)
-    for part in range(2):
-        gate_row[:, part * 1536 : (part + 1) * 1536] = jnp.dot(
-            chosen, gate_ref[:, cols(parity * NC + part * 1536, 1536)], preferred_element_type=F32
-        )
-
     kv_step(1, 0)
     w_got_near()
     kv_step(1, 1)
     for copy in q_local:
         copy.wait()
-    for d in (1, 3, 2):
-        for g in range(2):
-            arrived("QX%d%d" % (d, g), q_buf.at[g, rows(x_peers[4 - d] * ROWS, ROWS), :])
-
     def prepare(tile, g):
         for slot in (2 * tile, 2 * tile + 1):
             kv_from_sibling(slot, g)
@@ -284,10 +294,10 @@
 
     def service(i):
         todo = {
-            0: lambda: prepare(0, 0),
-            1: lambda: prepare(0, 1),
-            2: lambda: kv_step(2, 0),
-            3: lambda: kv_step(2, 1),
+            0: lambda: (q_wait(0, 0), prepare(0, 0)),
+            1: lambda: (q_wait(1, 0), prepare(0, 1)),
+            2: lambda: (kv_step(2, 0), q_wait(0, 1)),
+            3: lambda: (kv_step(2, 1), q_wait(1, 1)),
             4: lambda: prepare(1, 0),
             5: lambda: prepare(1, 1),
             6: lambda: kv_step(3, 0),
@@ -299,8 +309,13 @@
             13: lambda: prepare(3, 1),
             14: lambda: w_got_far(),
         }
-        for when, what in todo.items():
-            pl.when(i == when)(lambda what=what: (what(), None)[1])
+        def quarter(t):
+            for when, what in todo.items():
+                if when // 4 == t:
+                    pl.when(i == when)(lambda what=what: (what(), None)[1])
+
+        for t in range(4):
+            pl.when(i // 4 == t)(lambda t=t: quarter(t))
 
     def attend(i, carry):
         service(i)
@@ -337,12 +352,20 @@
                 h = side * 3 + j
                 a_st[g, side, :, j * HD : (j + 1) * HD] = (acc[g, h, :, 0:HD] / acc[g, h, :, HD : 2 * HD]).astype(BF16)
 
-        for when, what in {12: lambda: a_across(0), 13: lambda: a_across(1), 14: lambda: a_own(0), 15: lambda: a_own(1)}.items():
-            pl.when(i == when)(what)
+            for when, what in {12: lambda: a_across(0), 13: lambda: a_across(1), 14: lambda: a_own(0), 15: lambda: a_own(1)}.items():
+                pl.when(i == when)(what)
+
         return carry
 
     lax.fori_loop(0, 16, attend, 0)
 
+    chosen = (lax.broadcasted_iota(jnp.int32, (16, 64), 1) == levels_ref[span]).astype(F32).astype(BF16)
+    for part in range(2):
+        gate_row[:, part * 1536 : (part + 1) * 1536] = jnp.dot(
+            chosen, gate_ref[:, cols(parity * NC + part * 1536, 1536)], preferred_element_type=F32
+        )
+
+    drain("KX", "QX", "KR", "KL", "KS", "W")
     for g in range(2):
         a_forward(g)
     for g in range(2):
@@ -402,20 +425,21 @@
     project(0)
     y_got("YR", y_left)
     y_got("YL", y_right)
-    y_got("YF", y_far)
     w_from_sibling("YR", y_left)
     project(1)
+    pass_on(0)
     w_from_sibling("YL", y_right)
     project(2)
-    pass_on(0)
-    w_from_sibling("YF", y_far)
     pass_on(1)
     pass_on(2)
+    y_got("YF", y_far)
     for g in range(2):
         arrived("AZ%d" % g, a_place(1, 2 * b + g, z))
         arrived("AF%d" % g, a_place(1, 2 * (1 - b) + g, z))
-    for k in (4, 5, 6, 7):
+    for k in (4, 5, 6):
         project(k)
+    w_from_sibling("YF", y_far)
+    project(7)
     pass_on(4)
     project(3)
     finish(0)
@@ -425,26 +449,26 @@
     finish(2)
     pass_on(7)
     pass_on(3)
+    drain("A", "Y", "S", "RA", "LA")
     for k in (4, 5, 6, 7):
         finish(k)
     for k in range(4):
         take(k)
     finish(3)
-    for name, src, dst, where in sent:
-        message(name, src(), dst(), where()).wait_send()
+    drain("")
 
 
 def local(queries, key_value, w_out, gate_table, levels, span_mask, counts):
-    kv = jnp.transpose(key_value, (1, 0, 2))
     anywhere = pl.BlockSpec(memory_space=pl.ANY)
     vmem = pl.BlockSpec(memory_space=pltpu.VMEM)
     smem = pl.BlockSpec(memory_space=pltpu.SMEM)
     return pl.pallas_call(
         kernel,
         out_shape=jax.ShapeDtypeStruct((ROWS, D), BF16),
-        in_specs=[anywhere, anywhere, anywhere, vmem, smem, smem, smem],
+        in_specs=[anywhere, vmem, anywhere, vmem, smem, smem, smem],
         out_specs=vmem,
         scratch_shapes=[
+            pltpu.VMEM((2, ROWS, 1024), BF16),
             pltpu.VMEM((2, QT, 768), BF16),
             pltpu.VMEM((8, 2, 2, 2, QT, HD), BF16),
             pltpu.VMEM((2, 1024, HD), BF16),
@@ -469,7 +493,7 @@
         compiler_params=pltpu.CompilerParams(
             collective_id=0, has_side_effects=True, vmem_limit_bytes=56 * 1024 * 1024
         ),
-    )(queries, kv, w_out, gate_table, levels, span_mask, counts)
+    )(queries, key_value, w_out, gate_table, levels, span_mask, counts)
 
 
 def solution(mesh):

time: 98.4 us -> 94.3 us (0.958)
  local copies, waits for them, and re-layouts: 3.77 us -> 2.06 us
  Pallas kernels: 93.6 us -> 92.1 us
    unnamed x2 -> x1, local copies, waits for them, and re-layouts: 3.77 us -> 2.06 us
    pallas_call x1, Pallas kernels: 93.6 us -> 92.1 us  [local(): pl.pallas_call(kernel, out_shape=jax.ShapeDtypeStruct((ROWS, D), BF16), i...]
where the time goes in v3:
time: 94.3 us; the launch traced here: 94.2 us
  Pallas kernels  92.1 us (98%)
  local copies, waits for them, and re-layouts  2.06 us (2%)
    pallas_call x1, Pallas kernels, local(): pl.pallas_call(kernel, out_shape=jax.ShapeDtypeStruct((ROWS, D), BF16), i...  92.1 us
    unnamed x1, local copies, waits for them, and re-layouts  2.06 us

profile of v3, /device:TPU:1, one launch (start us, length us, event | category | flops | bytes accessed | tf_op | source)
XLA Modules:
  0.0 94.2 jit_solution(15087385542847610900)
XLA Ops:
  0.0 92.1 %shard_map.73 = bf16[64,6144]{1,0:T(8,128)(2,1)} custom-call(bf16[64,6144]{1,0:T(8,128)(2,1)} %q_hbm.1, bf16[64,2,1024]{2,1,0:T(2,128)(2,1)} %kv_ref.1, bf16[384,6144]{1,0:T(8,128)(2,1)} %w_hbm.1, bf16[64,6144]{1,0:T(8,128)(2,1)} %gate_ref.1, s32[4]{0:T(128)} %levels_ref.1, s32[4,4]{1,0:T(4,128)} %mask_ref.1, s32[4]{0:T(128)} %counts_ref.1), custom_call_target="tpu_custom_call" | custom-call | tf_op jit(solution)/shard_map/pallas_call | solution.py:465
  92.1 2.1 %copy.9 = bf16[64,6144]{1,0:T(8,128)(2,1)} copy(bf16[64,6144]{1,0:T(8,128)(2,1)} %shard_map.73) | data formatting | bytes 1572864

commit v4 on v3

--- a/solution.py
+++ b/solution.py
@@ -32,8 +32,8 @@
 
 
 def kernel(
-    q_hbm, kv_ref, w_hbm, gate_ref, levels_ref, mask_ref, counts_ref, out_ref,
-    kv_st, q_buf, kv_buf, kp, ve, m_ref, acc, a_st, a_buf, w_buf, o_st, ra_l, ra_r, rb_l, rb_r,
+    q_hbm, kv_ref, w_hbm, gate_hbm, levels_ref, mask_ref, counts_ref, out_ref,
+    gate_buf, kv_st, q_buf, kv_buf, kp, ve, m_ref, acc, a_st, a_buf, w_buf, o_st, ra_l, ra_r, rb_l, rb_r,
     f_out, f_in, gate_row, send_sem, recv_sem, local_sem,
 ):
     span = lax.axis_index("span")
@@ -97,8 +97,6 @@
         pl.semaphore_signal(barrier, inc=1, device_id=peer, device_id_type=MESH)
     kv_st[0] = kv_ref[:, 0, :]
     kv_st[1] = kv_ref[:, 1, :]
-    m_ref[...] = jnp.full(m_ref.shape, -1e30, F32)
-    acc[...] = jnp.zeros(acc.shape, F32)
     pl.semaphore_wait(barrier, len(peers))
 
     def group_of(xx, g):
@@ -141,22 +139,27 @@
         arrived("WL1", w_at(2 * SHARD, SHARD, y))
         y_out(2)
 
-    def w_sibling(name, n):
-        send("S" + name, lambda: w_at(SHARD, 3 * SHARD, n), lambda: w_at(SHARD, 3 * SHARD, n), lambda: sibling)
+    PARTS = {"A": (SHARD, 2 * SHARD), "B": (3 * SHARD, SHARD)}
+
+    def w_sibling(name, n, part):
+        start, size = PARTS[part]
+        send("S" + name + part, lambda: w_at(start, size, n), lambda: w_at(start, size, n), lambda: sibling)
 
     def w_from_sibling(name, n):
-        arrived("S" + name, w_at(SHARD, 3 * SHARD, n, 1 - core))
+        for part in PARTS:
+            start, size = PARTS[part]
+            arrived("S" + name + part, w_at(start, size, n, 1 - core))
 
     def w_got_far():
         arrived("WR2", w_at(3 * SHARD, half, y))
         arrived("WL2", w_at(3 * SHARD + half, half, y))
         y_out(3)
-        w_sibling("YO", y)
-
-    def y_got(way, n):
-        for slot in (1, 2, 3):
+        w_sibling("YO", y, "B")
+
+    def y_got(way, n, part):
+        for slot in (1, 2) if part == "A" else (3,):
             arrived("%s%d" % (way, slot), w_at(slot * SHARD, SHARD, n))
-        w_sibling(way, n)
+        w_sibling(way, n, part)
 
     def kv_sibling(slot, g):
         send("KS%d%d" % (slot, g), lambda: kv_buf.at[slot, 0, g], lambda: kv_buf.at[slot, 1, g], lambda: sibling)
@@ -240,7 +243,11 @@
         local_copy(2 + g, q_hbm.at[:, cols(group_of(x, g) * 768, 768)], q_buf.at[g, rows(x * ROWS, ROWS), :])
         for g in range(2)
     ]
+    gate_local = local_copy(7, gate_hbm.at[:, cols(parity * NC, NC)], gate_buf)
     w_local = local_copy(4, w_hbm.at[:, cols(parity * NC, NC)], w_buf.at[pl.ds(0, SHARD), :])
+
+    m_ref[...] = jnp.full(m_ref.shape, -1e30, F32)
+    acc[...] = jnp.zeros(acc.shape, F32)
 
     for g in range(2):
         kv_local[g].wait()
@@ -300,7 +307,7 @@
             3: lambda: (kv_step(2, 1), q_wait(1, 1)),
             4: lambda: prepare(1, 0),
             5: lambda: prepare(1, 1),
-            6: lambda: kv_step(3, 0),
+            6: lambda: (kv_step(3, 0), w_sibling("YO", y, "A")),
             7: lambda: kv_step(3, 1),
             8: lambda: (prepare(2, 0), w_far()),
             9: lambda: prepare(2, 1),
@@ -360,12 +367,15 @@
     lax.fori_loop(0, 16, attend, 0)
 
     chosen = (lax.broadcasted_iota(jnp.int32, (16, 64), 1) == levels_ref[span]).astype(F32).astype(BF16)
+    gate_local.wait()
     for part in range(2):
         gate_row[:, part * 1536 : (part + 1) * 1536] = jnp.dot(
-            chosen, gate_ref[:, cols(parity * NC + part * 1536, 1536)], preferred_element_type=F32
+            chosen, gate_buf[:, part * 1536 : (part + 1) * 1536], preferred_element_type=F32
         )
 
     drain("KX", "QX", "KR", "KL", "KS", "W")
+    y_got("YR", y_left, "A")
+    y_got("YL", y_right, "A")
     for g in range(2):
         a_forward(g)
     for g in range(2):
@@ -423,8 +433,9 @@
 
     w_from_sibling("YO", y)
     project(0)
-    y_got("YR", y_left)
-    y_got("YL", y_right)
+    y_got("YR", y_left, "B")
+    y_got("YL", y_right, "B")
+    y_got("YF", y_far, "A")
     w_from_sibling("YR", y_left)
     project(1)
     pass_on(0)
@@ -432,7 +443,7 @@
     project(2)
     pass_on(1)
     pass_on(2)
-    y_got("YF", y_far)
+    y_got("YF", y_far, "B")
     for g in range(2):
         arrived("AZ%d" % g, a_place(1, 2 * b + g, z))
         arrived("AF%d" % g, a_place(1, 2 * (1 - b) + g, z))
@@ -465,9 +476,10 @@
     return pl.pallas_call(
         kernel,
         out_shape=jax.ShapeDtypeStruct((ROWS, D), BF16),
-        in_specs=[anywhere, vmem, anywhere, vmem, smem, smem, smem],
+        in_specs=[anywhere, vmem, anywhere, anywhere, smem, smem, smem],
         out_specs=vmem,
         scratch_shapes=[
+            pltpu.VMEM((64, NC), BF16),
             pltpu.VMEM((2, ROWS, 1024), BF16),
             pltpu.VMEM((2, QT, 768), BF16),
             pltpu.VMEM((8, 2, 2, 2, QT, HD), BF16),

time: 94.3 us -> 94 us (level)
  no operation moved by 1% of the time
where the time goes in v4:
time: 94 us; the launch traced here: 93.9 us
  Pallas kernels  91.8 us (98%)
  local copies, waits for them, and re-layouts  2.06 us (2%)
    pallas_call x1, Pallas kernels, local(): pl.pallas_call(kernel, out_shape=jax.ShapeDtypeStruct((ROWS, D), BF16), i...  91.8 us
    unnamed x1, local copies, waits for them, and re-layouts  2.06 us

profile of v4, /device:TPU:1, one launch (start us, length us, event | category | flops | bytes accessed | tf_op | source)
XLA Modules:
  0.0 93.9 jit_solution(16271203806983074536)
XLA Ops:
  0.0 91.8 %shard_map.73 = bf16[64,6144]{1,0:T(8,128)(2,1)} custom-call(bf16[64,6144]{1,0:T(8,128)(2,1)} %q_hbm.1, bf16[64,2,1024]{2,1,0:T(2,128)(2,1)} %kv_ref.1, bf16[384,6144]{1,0:T(8,128)(2,1)} %w_hbm.1, bf16[64,6144]{1,0:T(8,128)(2,1)} %gate_hbm.1, s32[4]{0:T(128)} %levels_ref.1, s32[4,4]{1,0:T(4,128)} %mask_ref.1, s32[4]{0:T(128)} %counts_ref.1), custom_call_target="tpu_custom_call" | custom-call | tf_op jit(solution)/shard_map/pallas_call | solution.py:476
  91.8 2.1 %copy.9 = bf16[64,6144]{1,0:T(8,128)(2,1)} copy(bf16[64,6144]{1,0:T(8,128)(2,1)} %shard_map.73) | data formatting | bytes 1572864
